TPU v7x, 32 devices: a whole 2x2x4 slice. The times are simulated.
32 devices in a mesh: row: 8 (over z, x), sub: 4 (over y, core).
Axes of the slice: x: 2, y: 2, z: 4, core: 2. Of those that a mesh axis runs over, the one named last changes fastest.
Arguments:
- eig_vectors: float32 [65536, 512], P(('row', 'sub')), may hold values from -0.0234375 to 0.0234375
- vec_cotangent: float32 [65536, 512], P(('row', 'sub')), may hold values from -768 to 768
- levels: float32 [512], replicated, may hold values from -2 to 2
- order: int32 [512], replicated, may hold values from 0 to 511, each once
- neighbours: int32 [512, 12], P(('row', 'sub')), may hold values from 0 to 511, as said below
Outputs:
- grad_blocks: float32 [512, 12, 128, 128], P(('row', 'sub'))
Inputs may be any that keep to these rules, and one draw needn't show every extreme that they name: `neighbours`: entry 0 of row i is i itself. Row blocks are dealt to devices in order, 16 to a device, device index = row index * 4 + sub index; every listed block lies on the row block's own device or on a device whose row index or sub index (not both) differs by one, cyclically.
All inputs are finite; a program needn't handle non-finite values.
Results may differ from a plain program's by a relative error of at most 0.0003.
Values sent between devices are 32-bit elements; how exact they have to be, the bound alone decides.
A program may use at most 192 MiB of HBM per device.

v0:
```python
import jax
import jax.numpy as jnp
from jax import lax
from jax.sharding import PartitionSpec as P

BS = 128


broadening_sq = 0.0025


def with_halo(block, sides, width):
    for axis, dim in sides:
        count = lax.axis_size(axis)
        forward = [(i, i + 1) for i in range(count - 1)]
        forward.append((count - 1, 0))
        backward = [(target, source) for source, target in forward]
        low = lax.ppermute(
            lax.slice_in_dim(block, block.shape[dim] - width, None, axis=dim), axis, forward
        )
        high = lax.ppermute(lax.slice_in_dim(block, 0, width, axis=dim), axis, backward)
        block = jnp.concatenate([low, block, high], axis=dim)
    return block


def gap_rows(energy, row_energy):
    spread = energy[None, :] - row_energy[:, None]
    return spread / (spread * spread + broadening_sq)


def body(eig_vectors, vec_cotangent, levels, order, neighbours):
    highest = lax.Precision.HIGHEST
    window = eig_vectors.shape[1]
    local_rows = eig_vectors.shape[0]
    blk_count = local_rows // BS
    partial_value = lax.dot_general(
        eig_vectors,
        vec_cotangent,
        (((0,), (0,)), ((), ())),
        precision=highest,
        preferred_element_type=jnp.float32,
    )
    columns = lax.broadcasted_iota(jnp.int32, (window, window), 1)
    picker = (order[:, None] == columns).astype(jnp.float32)
    energy = jnp.dot(picker, levels, precision=highest, preferred_element_type=jnp.float32)
    gram = lax.psum(partial_value, ("row", "sub"))
    scaled = gap_rows(energy, energy) * gram
    adjoint_rows = jnp.dot(
        eig_vectors, scaled, precision=highest, preferred_element_type=jnp.float32
    )
    padded = with_halo(eig_vectors.reshape(1, 1, local_rows, window), (("row", 0), ("sub", 1)), 1)
    lookup_table = padded.reshape(9 * blk_count, BS, window)
    n_row = lax.axis_size("row")
    n_sub = lax.axis_size("sub")
    my_row = lax.axis_index("row")
    my_sub = lax.axis_index("sub")
    device = neighbours // blk_count
    local = neighbours % blk_count
    row_delta = (device // n_sub - my_row + n_row) % n_row
    sub_delta = (device % n_sub - my_sub + n_sub) % n_sub
    row_slot = 1 + (row_delta == 1).astype(jnp.int32) - (row_delta == n_row - 1).astype(jnp.int32)
    sub_slot = 1 + (sub_delta == 1).astype(jnp.int32) - (sub_delta == n_sub - 1).astype(jnp.int32)
    flat_index = (row_slot * 3 + sub_slot) * blk_count + local
    adj_blocks = adjoint_rows.reshape(blk_count, BS, window)

    def one_block(inputs_pair):
        adj_block, listed = inputs_pair
        picked = jnp.take(lookup_table, listed, axis=0)
        return jnp.einsum("ak,nbk->nab", adj_block, picked, precision=highest)

    return lax.map(one_block, (adj_blocks, flat_index))


def solution(mesh):
    in_specs = (P(("row", "sub"), None), P(("row", "sub"), None), P(), P(), P(("row", "sub"), None))
    out_specs = P(("row", "sub"), None, None, None)
    return jax.shard_map(body, mesh=mesh, in_specs=in_specs, out_specs=out_specs, check_vma=False)
```

profile of v0, /device:TPU:1, one launch (start us, length us, event | category | flops | bytes accessed | tf_op | source)
XLA Modules:
  0.0 665.0 jit_solution(3039789393281130007)
XLA Ops:
  11.7 176.3 %collective-permute-done = f32[1,1,2048,512]{3,2,1,0:T(8,128)S(1)} collective-permute-done((f32[1,1,2048,512]{3,2,1,0:T(8,128)}, f32[1,1,2048,512]{3,2,1,0:T(8,128)S(1)}, u32[]{:S(2)}, u32[]{:S(2)}) %collective-permute-start) | collective-permute-done | bytes 4194336 | tf_op jit(solution)/shard_map/ppermute | solution.py:18
  189.9 7.9 %pad_maximum_fusion.1 = f32[3,1,2048,512]{3,2,1,0:T(8,128)} fusion(f32[1,1,2048,512]{3,2,1,0:T(8,128)S(1)} %collective-permute-done.1, f32[1,1,2048,512]{3,2,1,0:T(8,128)} %bitcast.39, f32[1,1,2048,512]{3,2,1,0:T(8,128)S(1)} %collective-permute-done), kind=kLoop, calls=%fused_computation.18 | loop fusion | flops 6291456 | bytes 25165824 | tf_op jit(solution)/shard_map/concatenate | solution.py:22
  200.9 8.1 %fusion.30 = f32[512,512]{1,0:T(8,128)} fusion(f32[2048,512]{1,0:T(8,128)S(1)} %copy-done.2, f32[2048,512]{1,0:T(8,128)S(1)} %copy-done.5), kind=kOutput, calls=%fused_computation.58 | convolution fusion | flops 6442450944 | bytes 9437184 | tf_op jit(solution)/shard_map/dot_general | solution.py:36
  209.8 130.2 %all-reduce.2.cloned.1.call-done = f32[512,512]{1,0:T(8,128)} async-done(((f32[512,512]{1,0:T(8,128)}), f32[512,512]{1,0:T(8,128)}) %all-reduce.2.cloned.1.call-update) | async-done | bytes 1048592 | tf_op jit(solution)/shard_map/psum | solution.py:46
  340.0 16.9 %convolution_bitcast_fusion = f32[2048,512]{0,1:T(8,128)} fusion(f32[2048,512]{1,0:T(8,128)} %param.7, f32[512,512]{1,0:T(8,128)} %all-reduce.2.cloned.1.call-done, f32[512]{0:T(512)S(1)} %bitcast.42), kind=kOutput, calls=%fused_computation.19 | convolution fusion | flops 6443761664 | bytes 9439232 | tf_op jit(solution)/shard_map/dot_general | solution.py:48
  356.8 5.3 copy.8
  362.2 114.8 %collective-permute-done.2 = f32[3,1,2048,512]{3,2,1,0:T(8,128)} collective-permute-done((f32[3,1,2048,512]{3,2,1,0:T(8,128)}, f32[3,1,2048,512]{3,2,1,0:T(8,128)}, u32[]{:S(2)}, u32[]{:S(2)}) %collective-permute-start.2) | collective-permute-done | bytes 12582944 | tf_op jit(solution)/shard_map/ppermute | solution.py:18
  478.4 28.2 %pad_maximum_fusion = f32[3,3,2048,512]{3,2,1,0:T(8,128)} fusion(f32[3,1,2048,512]{3,2,1,0:T(8,128)} %collective-permute-done.3, f32[1,1,2048,512]{3,2,1,0:T(8,128)} %copy-done.4, f32[1,1,2048,512]{3,2,1,0:T(8,128)} %bitcast.40, f32[1,1,2048,512]{3,2,1,0:T(8,128)} %copy-done.3, f32[3,1,2048,512]{3,2,1,0:T(8,128)} %collective-permute-done.2), kind=kLoop, calls=%fused_computation.17 | loop fusion | flops 37748736 | bytes 75497472 | tf_op jit(solution)/shard_map/concatenate | solution.py:22
  506.6 150.9 %while.10 = (s32[]{:T(128)}, f32[16,12,128,128]{3,2,1,0:T(8,128)}, s32[16,12]{1,0:T(8,128)S(1)}, f32[144,128,512]{2,1,0:T(8,128)}, f32[16,128,512]{2,1,0:T(8,128)}, /*index=5*/s32[]{:T(128)}) while((s32[]{:T(128)}, f32[16,12,128,128]{3,2,1,0:T(8,128)}, s32[16,12]{1,0:T(8,128)S(1)}, f32[144,128,512]{2,1,0:T(8,128)}, f32[16,128,512]{2,1,0:T(8,128)}, ...), condition=%wide.region_2.3_spmd, body=%wide.region_1.2_spmd.sunk | while | flops 1208747136 | bytes 13636949 | solution.py:71
  518.6 4.5 fusion.42
  528.0 4.5 fusion.42
  537.5 4.5 fusion.42
  546.9 4.5 fusion.42
  556.3 4.5 fusion.42
  565.8 4.5 fusion.42
  575.2 4.5 fusion.42
  584.6 4.5 fusion.42
  594.1 4.5 fusion.42
  603.5 4.5 fusion.42
  612.9 4.5 fusion.42
  622.4 4.5 fusion.42
  631.8 4.5 fusion.42
  641.2 4.5 fusion.42
  650.7 4.5 fusion.42
  (124 shorter events, 96.3 us)
Async XLA Ops:
  6.5 202.5 %copy-start = (f32[512]{0:T(512)S(1)}, f32[512]{0:T(512)}, u32[]{:S(2)}) copy-start(f32[512]{0:T(512)} %param.9) | copy-start | bytes 6148
  6.5 333.4 %all-reduce.2.cloned.1.call-start = ((), (), s32[]{:S(2)}) async-start(), calls=%async_computation | async-start | bytes 2097152 | tf_op jit(solution)/shard_map/psum | solution.py:46
  6.5 194.4 %copy-start.2 = (f32[2048,512]{1,0:T(8,128)S(1)}, f32[2048,512]{1,0:T(8,128)}, u32[]{:S(2)}) copy-start(f32[2048,512]{1,0:T(8,128)} %param.7) | copy-start | bytes 12582916
  6.5 194.4 %copy-start.5 = (f32[2048,512]{1,0:T(8,128)S(1)}, f32[2048,512]{1,0:T(8,128)}, u32[]{:S(2)}) copy-start(f32[2048,512]{1,0:T(8,128)} %param.8) | copy-start | bytes 12582916
  6.5 181.5 %collective-permute-start = (f32[1,1,2048,512]{3,2,1,0:T(8,128)}, f32[1,1,2048,512]{3,2,1,0:T(8,128)S(1)}, u32[]{:S(2)}, u32[]{:S(2)}) collective-permute-start(f32[1,1,2048,512]{3,2,1,0:T(8,128)} %bitcast.37), channel_id=1, source_target_pairs={{0,4},{4,8},{8,12},{12,16},{16,20},{20,24},{24,28},{28,0},{1,5},{5... | collective-permute-start | bytes 12582920 | tf_op jit(solution)/shard_map/ppermute | solution.py:18
  8.6 181.2 %collective-permute-start.1 = (f32[1,1,2048,512]{3,2,1,0:T(8,128)}, f32[1,1,2048,512]{3,2,1,0:T(8,128)S(1)}, u32[]{:S(2)}, u32[]{:S(2)}) collective-permute-start(f32[1,1,2048,512]{3,2,1,0:T(8,128)} %bitcast.38), channel_id=1, source_target_pairs={{4,0},{8,4},{12,8},{16,12},{20,16},{24,20},{28,24},{0,28},{5,1},{9... | collective-permute-start | bytes 12582920 | tf_op jit(solution)/shard_map/ppermute | solution.py:21
  188.1 9.7 %copy-start.3 = (f32[1,1,2048,512]{3,2,1,0:T(8,128)}, f32[1,1,2048,512]{3,2,1,0:T(8,128)S(1)}, u32[]{:S(2)}) copy-start(f32[1,1,2048,512]{3,2,1,0:T(8,128)S(1)} %collective-permute-done) | copy-start | bytes 12582916
  189.9 8.0 %copy-start.4 = (f32[1,1,2048,512]{3,2,1,0:T(8,128)}, f32[1,1,2048,512]{3,2,1,0:T(8,128)S(1)}, u32[]{:S(2)}) copy-start(f32[1,1,2048,512]{3,2,1,0:T(8,128)S(1)} %collective-permute-done.1) | copy-start | bytes 12582916
  197.8 11.3 %copy-start.7 = (s32[512]{0:T(512)S(1)}, s32[512]{0:T(512)}, u32[]{:S(2)}) copy-start(s32[512]{0:T(512)} %param.10) | copy-start | bytes 6148
  197.8 11.9 %copy-start.6 = (s32[16,12]{1,0:T(8,128)S(1)}, s32[16,12]{1,0:T(8,128)}, u32[]{:S(2)}) copy-start(s32[16,12]{1,0:T(8,128)} %param.11) | copy-start | bytes 2308
  197.8 279.1 %collective-permute-start.2 = (f32[3,1,2048,512]{3,2,1,0:T(8,128)}, f32[3,1,2048,512]{3,2,1,0:T(8,128)}, u32[]{:S(2)}, u32[]{:S(2)}) collective-permute-start(f32[3,1,2048,512]{3,2,1,0:T(8,128)} %pad_maximum_fusion.1), channel_id=1, source_target_pairs={{0,1},{1,2},{2,3},{3,0},{4,5},{5,6},{6,7},{7,4},{8,9},{9,10},{10,1... | collective-permute-start | bytes 37748744 | tf_op jit(solution)/shard_map/ppermute | solution.py:18
  200.9 277.5 %collective-permute-start.3 = (f32[3,1,2048,512]{3,2,1,0:T(8,128)}, f32[3,1,2048,512]{3,2,1,0:T(8,128)}, u32[]{:S(2)}, u32[]{:S(2)}) collective-permute-start(f32[3,1,2048,512]{3,2,1,0:T(8,128)} %pad_maximum_fusion.1), channel_id=1, source_target_pairs={{1,0},{2,1},{3,2},{0,3},{5,4},{6,5},{7,6},{4,7},{9,8},{10,9},{11,1... | collective-permute-start | bytes 37748744 | tf_op jit(solution)/shard_map/ppermute | solution.py:21
  657.5 0.7 copy-start.1
Sparse Core Ops, SparseCore 0:
  209.2 130.7 all-reduce.1
where the time goes:
time: 667 us; the launch traced here: 665 us
  waiting for transfers between devices  425 us (64%)
  matrix products  97.3 us (15%)
  local copies, waits for them, and re-layouts  84.4 us (13%)
  other arithmetic  36.7 us (6%)
  between operations  13.5 us (2%)
  starting transfers between devices  8.31 us (1%)
    ppermute x2, waiting for transfers between devices, with_halo(): lax.ppermute(lax.slice_in_dim(block, block.shape[dim] - width, None, axis...  291 us
    psum x1, waiting for transfers between devices, body(): gram = lax.psum(partial_value, ('row', 'sub'))  130 us
    dot_general x16, matrix products, one_block(): return jnp.einsum('ak,nbk->nab', adj_block, picked, precision=highest)  71.8 us
    gather x16, local copies, waits for them, and re-layouts, one_block(): picked = jnp.take(lookup_table, listed, axis=0)  41 us
    dynamic_update_slice x32, local copies, waits for them, and re-layouts, body(): return lax.map(one_block, (adj_blocks, flat_index))  37.3 us
    concatenate x2, other arithmetic, with_halo(): block = jnp.concatenate([low, block, high], axis=dim)  36.1 us
    dot_general x1, matrix products, body(): jnp.dot(eig_vectors, scaled, precision=highest, preferred_element_type=jn...  16.9 us
  transfers between devices with their start and end apart: 5, of which 5 were waited for; matrix products, arithmetic and copies ran while one was open for 5% of the time, Pallas kernels for 0%

commit v1 on v0

v1 whole, which is shorter than its diff:
```python
import functools

import jax
import jax.numpy as jnp
from jax import lax
from jax.experimental import pallas as pl
from jax.experimental.pallas import tpu as pltpu
from jax.sharding import PartitionSpec as P

BS = 128
PIECE = 256
WIN = 3
LAG = 1

broadening_sq = 0.0025
MESH = pl.DeviceIdType.MESH
F32 = jnp.float32
BF16 = jnp.bfloat16


def split(x):
    hi = x.astype(BF16)
    return hi, (x - hi.astype(F32)).astype(BF16)


def mm(a, b, dims):
    return lax.dot_general(a, b, (dims, ((), ())), preferred_element_type=F32)


def stages_of(n_row, n_sub, window):
    stages = []
    length = window
    for axis, count in (("sub", n_sub), ("row", n_row)):
        mask = 1
        while mask < count:
            halve = length >= 16
            stages.append((axis, mask, length, halve))
            length = length // 2 if halve else length
            mask *= 2
    return stages, length


def halo_kernel(n_row, n_sub, stages, last,
                eig, cot, levels, order, table, wcat,
                qv, vv, acc, full, recv, sh, sl, wv,
                ld_sem, own_sem, w_sem, halo_send, halo_recv, ar_send, ar_recv):
    n_blk = eig.shape[0]
    window = eig.shape[2]
    row = lax.axis_index("row")
    sub = lax.axis_index("sub")
    odd = row % 2
    pair_row = row + 1 - 2 * odd
    ahead = (row + n_row + 2 - 4 * odd) % n_row
    behind = (row + n_row - 2 + 4 * odd) % n_row
    sub_up = (sub + 1) % n_sub
    sub_down = (sub + n_sub - 1) % n_sub

    def flip(axis, mask):
        here = row if axis == "row" else sub
        bit = (here // mask) % 2
        there = here + mask - 2 * mask * bit
        return ((there, sub) if axis == "row" else (row, there)), bit

    partners = [(row, sub_up), (row, sub_down), (pair_row, sub), (ahead, sub), (behind, sub)]
    for axis, mask, _, _ in stages:
        if (axis, mask) not in (("sub", 1), ("row", 1)):
            partners.append(flip(axis, mask)[0])
    barrier = pltpu.get_barrier_semaphore()

    per = PIECE // BS
    n_piece = n_blk // per

    def load(p, which):
        src, dst = ((eig, qv), (cot, vv))[which]
        at = pl.ds(p * per, per)
        return pltpu.make_async_copy(src.at[at], dst.at[at], ld_sem.at[which, p])

    for p in range(n_piece):
        load(p, 0).start()
        load(p, 1).start()
    own = pltpu.make_async_copy(eig, table.at[pl.ds(0, n_blk)], own_sem)
    own.start()

    for there in partners:
        pl.semaphore_signal(barrier, inc=1, device_id=there, device_id_type=MESH)
    pl.semaphore_wait(barrier, len(partners))

    def halo(way, t):
        dev = ((row, sub_up), (row, sub_down), (pair_row, sub), (ahead, sub))[way]
        src = table.at[3 * n_blk + t] if way == 3 else eig.at[t]
        return pltpu.make_async_remote_copy(
            src_ref=src, dst_ref=table.at[(way + 1) * n_blk + t],
            send_sem=halo_send.at[way, t], recv_sem=halo_recv.at[way, t],
            device_id=dev, device_id_type=MESH)

    def gram():
        acc[...] = jnp.zeros_like(acc)

        def body(p, carry):
            load(p, 0).wait()
            load(p, 1).wait()
            at = pl.ds(p * per, per)
            qh, ql = split(qv[at].reshape(PIECE, window))
            vh, vl = split(vv[at].reshape(PIECE, window))
            d = ((0,), (0,))
            acc[...] += mm(qh, vh, d) + (mm(qh, vl, d) + mm(ql, vh, d))
            return carry

        lax.fori_loop(0, n_piece, body, 0)

    offs = [0 * row]
    for axis, mask, length, halve in stages:
        _, bit = flip(axis, mask)
        offs.append(offs[-1] + bit * (length // 2) if halve else offs[-1])
    spans = [s[2] for s in stages] + [last]
    rec_at = [sum(s[2] // 2 if s[3] else s[2] for s in stages[:k]) for k in range(len(stages))]

    def scatter(k):
        axis, mask, length, halve = stages[k]
        dev, bit = flip(axis, mask)
        size = length // 2 if halve else length
        out = offs[k] + (1 - bit) * size if halve else offs[k]
        return pltpu.make_async_remote_copy(
            src_ref=acc.at[pl.ds(pl.multiple_of(out, 8), size)],
            dst_ref=recv.at[pl.ds(rec_at[k], size)],
            send_sem=ar_send.at[0, k], recv_sem=ar_recv.at[0, k],
            device_id=dev, device_id_type=MESH), size

    def scatter_end(k):
        copy, size = scatter(k)
        copy.wait()
        keep = pl.ds(pl.multiple_of(offs[k + 1], 8), size)
        acc[keep] = acc[keep] + recv[pl.ds(rec_at[k], size)]

    def gather(k):
        dev, _ = flip(stages[k][0], stages[k][1])
        at = pl.ds(pl.multiple_of(offs[k + 1], 8), spans[k + 1])
        return pltpu.make_async_remote_copy(
            src_ref=full.at[at], dst_ref=full.at[at],
            send_sem=ar_send.at[1, k], recv_sem=ar_recv.at[1, k],
            device_id=dev, device_id_type=MESH)

    def gather_end(k):
        dev, bit = flip(stages[k][0], stages[k][1])
        copy = gather(k)
        copy.wait_send()
        copy.wait_recv()

    def scale():
        lev = jnp.broadcast_to(levels[...], (window, window)).T
        slot = lax.broadcasted_iota(jnp.int32, (window, window), 0)
        energy = jnp.sum(jnp.where(slot == order[...], lev, 0.0), axis=0, keepdims=True)
        upper = jnp.broadcast_to(energy, (window, window))
        spread = upper - upper.T
        hi, lo = split(spread / (spread * spread + broadening_sq) * full[...])
        sh[...] = hi
        sl[...] = lo

    def adjoint(first, count):
        def body(p, carry):
            qh, ql = split(qv[pl.ds(p * per, per)].reshape(PIECE, window))
            d = ((1,), (0,))
            wh, wl = split(mm(qh, sh[...], d) + (mm(qh, sl[...], d) + mm(ql, sh[...], d)))
            wv[pl.ds(p * per, per), 0] = wh.reshape(per, BS, window)
            wv[pl.ds(p * per, per), 1] = wl.reshape(per, BS, window)
            return carry

        lax.fori_loop(first, first + count, body, 0)

    rounds = [k for k in range(len(stages)) if stages[k][3]]
    jobs = [lambda: None, lambda: None, gram]

    def begin():
        scatter(0)[0].start()

    def middle(k):
        scatter_end(k)
        scatter(k + 1)[0].start()

    def turn():
        scatter_end(len(stages) - 1)
        at = pl.ds(pl.multiple_of(offs[-1], 8), last)
        full[at] = acc[at]
        gather(rounds[-1]).start()

    def back(k, after):
        gather_end(k)
        gather(after).start()

    def finish():
        gather_end(rounds[0])
        scale()

    jobs.append(begin)
    for k in range(len(stages) - 1):
        jobs.append(functools.partial(middle, k))
    jobs.append(turn)
    for k, after in zip(rounds[::-1][:-1], rounds[::-1][1:]):
        jobs.append(functools.partial(back, k, after))
    jobs.append(finish)
    jobs.append(functools.partial(adjoint, 0, n_piece // 2))
    jobs.append(functools.partial(adjoint, n_piece // 2, n_piece - n_piece // 2))

    for t in range(max(n_blk + LAG, len(jobs))):
        if t < n_blk:
            if t >= WIN:
                for way in (0, 1, 2):
                    halo(way, t - WIN).wait_send()
            for way in (2, 0, 1):
                halo(way, t).start()
        if LAG <= t < n_blk + LAG:
            if t >= LAG + WIN:
                halo(3, t - LAG - WIN).wait_send()
            halo(2, t - LAG).wait_recv()
            halo(3, t - LAG).start()
        if t < len(jobs):
            jobs[t]()

    put = pltpu.make_async_copy(wv, wcat, w_sem)
    put.start()
    for t in range(n_blk):
        for way in (0, 1, 3):
            halo(way, t).wait_recv()
    for t in range(n_blk - WIN, n_blk):
        for way in (0, 1, 2, 3):
            halo(way, t).wait_send()
    own.wait()
    put.wait()


def block_kernel(listed, wcat, table, out, buf, sem):
    i = pl.program_id(0)
    n = pl.num_programs(0)
    n_nbr = buf.shape[1]
    window = table.shape[2]

    def fetch(step, k):
        slot = step % 2
        return pltpu.make_async_copy(table.at[listed[step, k]], buf.at[slot, k], sem.at[slot, k])

    @pl.when(i == 0)
    def _():
        for k in range(n_nbr):
            fetch(0, k).start()

    @pl.when(i + 1 < n)
    def _():
        for k in range(n_nbr):
            fetch(i + 1, k).start()

    both = wcat[0].reshape(2 * BS, window)
    d = ((1,), (1,))
    for k in range(0, n_nbr, 2):
        fetch(i, k).wait()
        fetch(i, k + 1).wait()
        qh, ql = split(buf[i % 2, pl.ds(k, 2)].reshape(2 * BS, window))
        big = mm(both, qh, d)
        res = big[:BS] + (big[BS:] + mm(both[:BS], ql, d))
        out[0, k] = res[:, :BS]
        out[0, k + 1] = res[:, BS:]


def body(n_row, n_sub, eig_vectors, vec_cotangent, levels, order, neighbours):
    rows, window = eig_vectors.shape
    n_blk = rows // BS
    n_nbr = neighbours.shape[1]
    eig = eig_vectors.reshape(n_blk, BS, window)
    cot = vec_cotangent.reshape(n_blk, BS, window)
    stages, last = stages_of(n_row, n_sub, window)
    n_rec = sum(s[2] // 2 if s[3] else s[2] for s in stages)
    any_spec = pl.BlockSpec(memory_space=pl.ANY)
    vmem_spec = pl.BlockSpec(memory_space=pltpu.VMEM)
    n_st = len(stages)
    table, wcat = pl.pallas_call(
        functools.partial(halo_kernel, n_row, n_sub, stages, last),
        out_shape=[
            jax.ShapeDtypeStruct((5 * n_blk, BS, window), F32),
            jax.ShapeDtypeStruct((n_blk, 2, BS, window), BF16),
        ],
        in_specs=[any_spec, any_spec, vmem_spec, vmem_spec],
        out_specs=[any_spec, any_spec],
        scratch_shapes=[
            pltpu.VMEM((n_blk, BS, window), F32),
            pltpu.VMEM((n_blk, BS, window), F32),
            pltpu.VMEM((window, window), F32),
            pltpu.VMEM((window, window), F32),
            pltpu.VMEM((n_rec, window), F32),
            pltpu.VMEM((window, window), BF16),
            pltpu.VMEM((window, window), BF16),
            pltpu.VMEM((n_blk, 2, BS, window), BF16),
            pltpu.SemaphoreType.DMA((2, rows // PIECE)),
            pltpu.SemaphoreType.DMA,
            pltpu.SemaphoreType.DMA,
            pltpu.SemaphoreType.DMA((4, n_blk)),
            pltpu.SemaphoreType.DMA((4, n_blk)),
            pltpu.SemaphoreType.DMA((2, n_st)),
            pltpu.SemaphoreType.DMA((2, n_st)),
        ],
        compiler_params=pltpu.CompilerParams(
            collective_id=0, has_side_effects=True, vmem_limit_bytes=48 * 2**20),
        name="halo",
    )(eig, cot, levels.reshape(1, window), order.reshape(1, window))

    my_row = lax.axis_index("row")
    my_sub = lax.axis_index("sub")
    device = neighbours // n_blk
    dev_row = device // n_sub
    dev_sub = device % n_sub
    pair_row = my_row + 1 - 2 * (my_row % 2)
    up = (my_sub + 1) % n_sub
    same_row = jnp.where(dev_sub == my_sub, 0, jnp.where(dev_sub == up, 2, 1))
    slot = jnp.where(dev_row == my_row, same_row, jnp.where(dev_row == pair_row, 3, 4))
    listed = slot * n_blk + neighbours % n_blk

    return pl.pallas_call(
        block_kernel,
        out_shape=jax.ShapeDtypeStruct((n_blk, n_nbr, BS, BS), F32),
        grid_spec=pltpu.PrefetchScalarGridSpec(
            num_scalar_prefetch=1,
            grid=(n_blk,),
            in_specs=[
                pl.BlockSpec((1, 2, BS, window), lambda i, listed: (i, 0, 0, 0)),
                any_spec,
            ],
            out_specs=pl.BlockSpec((1, n_nbr, BS, BS), lambda i, listed: (i, 0, 0, 0)),
            scratch_shapes=[
                pltpu.VMEM((2, n_nbr, BS, window), F32),
                pltpu.SemaphoreType.DMA((2, n_nbr)),
            ],
        ),
        compiler_params=pltpu.CompilerParams(vmem_limit_bytes=48 * 2**20),
        name="blocks",
    )(listed.astype(jnp.int32), wcat, table)


def solution(mesh):
    in_specs = (P(("row", "sub"), None), P(("row", "sub"), None), P(), P(), P(("row", "sub"), None))
    out_specs = P(("row", "sub"), None, None, None)
    run = functools.partial(body, mesh.shape["row"], mesh.shape["sub"])
    return jax.shard_map(run, mesh=mesh, in_specs=in_specs, out_specs=out_specs, check_vma=False)
```

time: 667 us -> 177 us (0.27)
  waiting for transfers between devices: 425 us -> 0 us
  Pallas kernels: 0 us -> 174 us
  matrix products: 97.3 us -> 0 us
  local copies, waits for them, and re-layouts: 84.4 us -> 1.36 us
  other arithmetic: 36.7 us -> 0.72 us
  between operations: 13.5 us -> 0.02 us
  starting transfers between devices: 8.31 us -> 0 us
    ppermute x4 -> x0, waiting for transfers between devices: 294 us -> none  [the longest x2 291 us: with_halo(): lax.ppermute(lax.slice_in_dim(block, block.shape[dim] - width, None, axis...]
    pallas_call x0 -> x2, Pallas kernels: none -> 174 us  [the longest x1 130 us: body(): pl.pallas_call(functools.partial(halo_kernel, n_row, n_sub, stages, last)...]
    psum x1 -> x0, waiting for transfers between devices: 130 us -> none  [body(): gram = lax.psum(partial_value, ('row', 'sub'))]
    dot_general x19 -> x0, matrix products: 97.3 us -> none  [the longest x16 71.8 us: one_block(): return jnp.einsum('ak,nbk->nab', adj_block, picked, precision=highest)]
    gather x16 -> x0, local copies, waits for them, and re-layouts: 41 us -> none  [one_block(): picked = jnp.take(lookup_table, listed, axis=0)]
    dynamic_update_slice x32 -> x0, local copies, waits for them, and re-layouts: 37.3 us -> none  [body(): return lax.map(one_block, (adj_blocks, flat_index))]
    concatenate x2 -> x0, other arithmetic: 36.1 us -> none  [with_halo(): block = jnp.concatenate([low, block, high], axis=dim)]
    ppermute x4 -> x0, starting transfers between devices: 8.31 us -> none  [the longest x2 5.2 us: with_halo(): lax.ppermute(lax.slice_in_dim(block, block.shape[dim] - width, None, axis...]
  transfers between devices with their start and end apart: 5 -> 0, of which waited for: 5 -> 0; matrix products, arithmetic and copies ran while one was open for 5% -> 0% of each run, Pallas kernels for 0% -> 0%
where the time goes in v1:
time: 177 us; the launch traced here: 176 us
  Pallas kernels  174 us (98%)
    pallas_call x1, Pallas kernels, body(): pl.pallas_call(functools.partial(halo_kernel, n_row, n_sub, stages, last)...  130 us
    pallas_call x1, Pallas kernels, body(): pl.pallas_call(block_kernel, out_shape=jax.ShapeDtypeStruct((n_blk, n_nbr...  44.5 us

profile of v1, /device:TPU:1, one launch (start us, length us, event | category | flops | bytes accessed | tf_op | source)
XLA Modules:
  0.0 176.3 jit_solution(9584145865273419532)
XLA Ops:
  0.0 0.7 fusion.listed
  0.7 0.0 copy-start
  0.7 0.7 copy-done
  1.4 0.0 copy-start.1
  1.4 0.7 copy-done.1
  2.1 129.7 %halo.1 = (f32[80,128,512]{2,1,0:T(8,128)}, bf16[16,2,128,512]{3,2,1,0:T(8,128)(2,1)S(1)}) custom-call(f32[16,128,512]{2,1,0:T(8,128)} %bitcast.6, f32[16,128,512]{2,1,0:T(8,128)} %bitcast.7, f32[1,512]{1,0:T(1,128)S(1)} %bitcast.4, s32[1,512]{1,0:T(1,128)S(1)} %bitcast.5), custom_call_target="tpu_custom_call" | custom-call | tf_op jit(solution)/shard_map/halo/pallas_call | solution.py:274
  131.8 44.5 %blocks.1 = f32[16,12,128,128]{3,2,1,0:T(8,128)} custom-call(s32[16,12]{1,0:T(8,128)S(1)} %fusion.listed, bf16[16,2,128,512]{3,2,1,0:T(8,128)(2,1)S(1)} %get-tuple-element.7.wcat, f32[80,128,512]{2,1,0:T(8,128)} %get-tuple-element.8.table), custom_call_target="tpu_custom_call" | custom-call | tf_op jit(solution)/shard_map/blocks/pallas_call | solution.py:315
Async XLA Ops:
  0.7 0.7 copy-start
  1.4 0.7 copy-start.1

commit v2 on v1

--- a/solution.py
+++ b/solution.py
@@ -9,8 +9,10 @@
 
 BS = 128
 PIECE = 256
-WIN = 3
+CHUNK = 64
+WIN = 4
 LAG = 1
+GAP = 2
 
 broadening_sq = 0.0025
 MESH = pl.DeviceIdType.MESH
@@ -44,7 +46,7 @@
                 eig, cot, levels, order, table, wcat,
                 qv, vv, acc, full, recv, sh, sl, wv,
                 ld_sem, own_sem, w_sem, halo_send, halo_recv, ar_send, ar_recv):
-    n_blk = eig.shape[0]
+    n_chunk = eig.shape[0]
     window = eig.shape[2]
     row = lax.axis_index("row")
     sub = lax.axis_index("sub")
@@ -67,8 +69,9 @@
             partners.append(flip(axis, mask)[0])
     barrier = pltpu.get_barrier_semaphore()
 
-    per = PIECE // BS
-    n_piece = n_blk // per
+    per = PIECE // CHUNK
+    blocks = PIECE // BS
+    n_piece = n_chunk // per
 
     def load(p, which):
         src, dst = ((eig, qv), (cot, vv))[which]
@@ -78,7 +81,7 @@
     for p in range(n_piece):
         load(p, 0).start()
         load(p, 1).start()
-    own = pltpu.make_async_copy(eig, table.at[pl.ds(0, n_blk)], own_sem)
+    own = pltpu.make_async_copy(eig, table.at[pl.ds(0, n_chunk)], own_sem)
     own.start()
 
     for there in partners:
@@ -87,9 +90,9 @@
 
     def halo(way, t):
         dev = ((row, sub_up), (row, sub_down), (pair_row, sub), (ahead, sub))[way]
-        src = table.at[3 * n_blk + t] if way == 3 else eig.at[t]
+        src = table.at[3 * n_chunk + t] if way == 3 else eig.at[t]
         return pltpu.make_async_remote_copy(
-            src_ref=src, dst_ref=table.at[(way + 1) * n_blk + t],
+            src_ref=src, dst_ref=table.at[(way + 1) * n_chunk + t],
             send_sem=halo_send.at[way, t], recv_sem=halo_recv.at[way, t],
             device_id=dev, device_id_type=MESH)
 
@@ -160,16 +163,16 @@
         def body(p, carry):
             qh, ql = split(qv[pl.ds(p * per, per)].reshape(PIECE, window))
             d = ((1,), (0,))
-            wh, wl = split(mm(qh, sh[...], d) + (mm(qh, sl[...], d) + mm(ql, sh[...], d)))
-            wv[pl.ds(p * per, per), 0] = wh.reshape(per, BS, window)
-            wv[pl.ds(p * per, per), 1] = wl.reshape(per, BS, window)
+            w = mm(qh, sh[...], d) + (mm(qh, sl[...], d) + mm(ql, sh[...], d))
+            for b in range(blocks):
+                hi, lo = split(w[b * BS:(b + 1) * BS].T)
+                wv[p * blocks + b, :, :BS] = hi
+                wv[p * blocks + b, :, BS:] = lo
             return carry
 
         lax.fori_loop(first, first + count, body, 0)
 
     rounds = [k for k in range(len(stages)) if stages[k][3]]
-    jobs = [lambda: None, lambda: None, gram]
-
     def begin():
         scatter(0)[0].start()
 
@@ -191,37 +194,42 @@
         gather_end(rounds[0])
         scale()
 
-    jobs.append(begin)
+    jobs = {WIN - 1: gram, WIN: begin}
+    at_step = WIN + GAP
     for k in range(len(stages) - 1):
-        jobs.append(functools.partial(middle, k))
-    jobs.append(turn)
+        jobs[at_step] = functools.partial(middle, k)
+        at_step += GAP
+    jobs[at_step] = turn
+    at_step += GAP
     for k, after in zip(rounds[::-1][:-1], rounds[::-1][1:]):
-        jobs.append(functools.partial(back, k, after))
-    jobs.append(finish)
-    jobs.append(functools.partial(adjoint, 0, n_piece // 2))
-    jobs.append(functools.partial(adjoint, n_piece // 2, n_piece - n_piece // 2))
-
-    for t in range(max(n_blk + LAG, len(jobs))):
-        if t < n_blk:
+        jobs[at_step] = functools.partial(back, k, after)
+        at_step += GAP
+    jobs[at_step] = finish
+    for p in range(0, n_piece, 2):
+        at_step += 1
+        jobs[at_step] = functools.partial(adjoint, p, 2)
+
+    for t in range(max(n_chunk + LAG, max(jobs) + 1)):
+        if t < n_chunk:
             if t >= WIN:
                 for way in (0, 1, 2):
                     halo(way, t - WIN).wait_send()
             for way in (2, 0, 1):
                 halo(way, t).start()
-        if LAG <= t < n_blk + LAG:
+        if LAG <= t < n_chunk + LAG:
             if t >= LAG + WIN:
                 halo(3, t - LAG - WIN).wait_send()
             halo(2, t - LAG).wait_recv()
             halo(3, t - LAG).start()
-        if t < len(jobs):
+        if t in jobs:
             jobs[t]()
 
     put = pltpu.make_async_copy(wv, wcat, w_sem)
     put.start()
-    for t in range(n_blk):
+    for t in range(n_chunk):
         for way in (0, 1, 3):
             halo(way, t).wait_recv()
-    for t in range(n_blk - WIN, n_blk):
+    for t in range(n_chunk - WIN, n_chunk):
         for way in (0, 1, 2, 3):
             halo(way, t).wait_send()
     own.wait()
@@ -248,24 +256,25 @@
         for k in range(n_nbr):
             fetch(i + 1, k).start()
 
-    both = wcat[0].reshape(2 * BS, window)
-    d = ((1,), (1,))
-    for k in range(0, n_nbr, 2):
-        fetch(i, k).wait()
-        fetch(i, k + 1).wait()
-        qh, ql = split(buf[i % 2, pl.ds(k, 2)].reshape(2 * BS, window))
-        big = mm(both, qh, d)
-        res = big[:BS] + (big[BS:] + mm(both[:BS], ql, d))
-        out[0, k] = res[:, :BS]
-        out[0, k + 1] = res[:, BS:]
+    d = ((1,), (0,))
+    group = n_nbr // 2
+    for first in range(0, n_nbr, group):
+        for k in range(first, first + group):
+            fetch(i, k).wait()
+        qh, ql = split(buf[i % 2, pl.ds(first, group)].reshape(group * BS, window))
+        big = mm(qh, wcat[0], d)
+        res = big[:, :BS] + (big[:, BS:] + mm(ql, wcat[0, :, :BS], d))
+        for k in range(group):
+            out[0, first + k] = res[k * BS:(k + 1) * BS].T
 
 
 def body(n_row, n_sub, eig_vectors, vec_cotangent, levels, order, neighbours):
     rows, window = eig_vectors.shape
     n_blk = rows // BS
     n_nbr = neighbours.shape[1]
-    eig = eig_vectors.reshape(n_blk, BS, window)
-    cot = vec_cotangent.reshape(n_blk, BS, window)
+    n_chunk = rows // CHUNK
+    eig = eig_vectors.reshape(n_chunk, CHUNK, window)
+    cot = vec_cotangent.reshape(n_chunk, CHUNK, window)
     stages, last = stages_of(n_row, n_sub, window)
     n_rec = sum(s[2] // 2 if s[3] else s[2] for s in stages)
     any_spec = pl.BlockSpec(memory_space=pl.ANY)
@@ -274,25 +283,25 @@
     table, wcat = pl.pallas_call(
         functools.partial(halo_kernel, n_row, n_sub, stages, last),
         out_shape=[
-            jax.ShapeDtypeStruct((5 * n_blk, BS, window), F32),
-            jax.ShapeDtypeStruct((n_blk, 2, BS, window), BF16),
+            jax.ShapeDtypeStruct((5 * n_chunk, CHUNK, window), F32),
+            jax.ShapeDtypeStruct((n_blk, window, 2 * BS), BF16),
         ],
         in_specs=[any_spec, any_spec, vmem_spec, vmem_spec],
         out_specs=[any_spec, any_spec],
         scratch_shapes=[
-            pltpu.VMEM((n_blk, BS, window), F32),
-            pltpu.VMEM((n_blk, BS, window), F32),
+            pltpu.VMEM((n_chunk, CHUNK, window), F32),
+            pltpu.VMEM((n_chunk, CHUNK, window), F32),
             pltpu.VMEM((window, window), F32),
             pltpu.VMEM((window, window), F32),
             pltpu.VMEM((n_rec, window), F32),
             pltpu.VMEM((window, window), BF16),
             pltpu.VMEM((window, window), BF16),
-            pltpu.VMEM((n_blk, 2, BS, window), BF16),
+            pltpu.VMEM((n_blk, window, 2 * BS), BF16),
             pltpu.SemaphoreType.DMA((2, rows // PIECE)),
             pltpu.SemaphoreType.DMA,
             pltpu.SemaphoreType.DMA,
-            pltpu.SemaphoreType.DMA((4, n_blk)),
-            pltpu.SemaphoreType.DMA((4, n_blk)),
+            pltpu.SemaphoreType.DMA((4, n_chunk)),
+            pltpu.SemaphoreType.DMA((4, n_chunk)),
             pltpu.SemaphoreType.DMA((2, n_st)),
             pltpu.SemaphoreType.DMA((2, n_st)),
         ],
@@ -319,7 +328,7 @@
             num_scalar_prefetch=1,
             grid=(n_blk,),
             in_specs=[
-                pl.BlockSpec((1, 2, BS, window), lambda i, listed: (i, 0, 0, 0)),
+                pl.BlockSpec((1, window, 2 * BS), lambda i, listed: (i, 0, 0)),
                 any_spec,
             ],
             out_specs=pl.BlockSpec((1, n_nbr, BS, BS), lambda i, listed: (i, 0, 0, 0)),
@@ -330,7 +339,7 @@
         ),
         compiler_params=pltpu.CompilerParams(vmem_limit_bytes=48 * 2**20),
         name="blocks",
-    )(listed.astype(jnp.int32), wcat, table)
+    )(listed.astype(jnp.int32), wcat, table.reshape(5 * n_blk, BS, window))
 
 
 def solution(mesh):

time: 177 us -> 162 us (0.915)
  Pallas kernels: 174 us -> 159 us
    pallas_call x1, Pallas kernels: 44.5 us -> 28.2 us  [body(): pl.pallas_call(block_kernel, out_shape=jax.ShapeDtypeStruct((n_blk, n_nbr...]
where the time goes in v2:
time: 162 us; the launch traced here: 161 us
  Pallas kernels  159 us (98%)
    pallas_call x1, Pallas kernels, body(): pl.pallas_call(functools.partial(halo_kernel, n_row, n_sub, stages, last)...  131 us
    pallas_call x1, Pallas kernels, body(): pl.pallas_call(block_kernel, out_shape=jax.ShapeDtypeStruct((n_blk, n_nbr...  28.2 us

profile of v2, /device:TPU:1, one launch (start us, length us, event | category | flops | bytes accessed | tf_op | source)
XLA Modules:
  0.0 161.1 jit_solution(3852870958111236162)
XLA Ops:
  0.0 0.7 fusion.listed
  0.7 0.0 copy-start
  0.7 0.7 copy-done
  1.4 0.0 copy-start.1
  1.4 0.7 copy-done.1
  2.1 130.8 %halo.1 = (f32[160,64,512]{2,1,0:T(8,128)}, bf16[16,512,256]{2,1,0:T(8,128)(2,1)S(1)}) custom-call(f32[32,64,512]{2,1,0:T(8,128)} %bitcast.8, f32[32,64,512]{2,1,0:T(8,128)} %bitcast.9, f32[1,512]{1,0:T(1,128)S(1)} %bitcast.5, s32[1,512]{1,0:T(1,128)S(1)} %bitcast.6), custom_call_target="tpu_custom_call" | custom-call | tf_op jit(solution)/shard_map/halo/pallas_call | solution.py:283
  132.9 28.2 %blocks.1 = f32[16,12,128,128]{3,2,1,0:T(8,128)} custom-call(s32[16,12]{1,0:T(8,128)S(1)} %fusion.listed, bf16[16,512,256]{2,1,0:T(8,128)(2,1)S(1)} %get-tuple-element.7.wcat, f32[80,128,512]{2,1,0:T(8,128)} %bitcast.7), custom_call_target="tpu_custom_call" | custom-call | tf_op jit(solution)/shard_map/blocks/pallas_call | solution.py:324
Async XLA Ops:
  0.7 0.7 copy-start
  1.4 0.7 copy-start.1

commit v3 on v2

--- a/solution.py
+++ b/solution.py
@@ -10,8 +10,8 @@
 BS = 128
 PIECE = 256
 CHUNK = 64
-WIN = 4
-LAG = 1
+WIN = 6
+LAG = 4
 GAP = 2
 
 broadening_sq = 0.0025
@@ -84,6 +84,7 @@
     own = pltpu.make_async_copy(eig, table.at[pl.ds(0, n_chunk)], own_sem)
     own.start()
 
+    acc[...] = jnp.zeros_like(acc)
     for there in partners:
         pl.semaphore_signal(barrier, inc=1, device_id=there, device_id_type=MESH)
     pl.semaphore_wait(barrier, len(partners))
@@ -96,9 +97,7 @@
             send_sem=halo_send.at[way, t], recv_sem=halo_recv.at[way, t],
             device_id=dev, device_id_type=MESH)
 
-    def gram():
-        acc[...] = jnp.zeros_like(acc)
-
+    def gram(first, count):
         def body(p, carry):
             load(p, 0).wait()
             load(p, 1).wait()
@@ -109,7 +108,7 @@
             acc[...] += mm(qh, vh, d) + (mm(qh, vl, d) + mm(ql, vh, d))
             return carry
 
-        lax.fori_loop(0, n_piece, body, 0)
+        lax.fori_loop(first, first + count, body, 0)
 
     offs = [0 * row]
     for axis, mask, length, halve in stages:
@@ -194,8 +193,13 @@
         gather_end(rounds[0])
         scale()
 
-    jobs = {WIN - 1: gram, WIN: begin}
-    at_step = WIN + GAP
+    jobs = {}
+    at_step = LAG
+    for p in range(0, n_piece, 2):
+        jobs[at_step] = functools.partial(gram, p, 2)
+        at_step += 1
+    jobs[at_step] = begin
+    at_step += GAP
     for k in range(len(stages) - 1):
         jobs[at_step] = functools.partial(middle, k)
         at_step += GAP
@@ -257,10 +261,10 @@
             fetch(i + 1, k).start()
 
     d = ((1,), (0,))
-    group = n_nbr // 2
+    for k in range(n_nbr):
+        fetch(i, k).wait()
+    group = 4
     for first in range(0, n_nbr, group):
-        for k in range(first, first + group):
-            fetch(i, k).wait()
         qh, ql = split(buf[i % 2, pl.ds(first, group)].reshape(group * BS, window))
         big = mm(qh, wcat[0], d)
         res = big[:, :BS] + (big[:, BS:] + mm(ql, wcat[0, :, :BS], d))

time: 162 us -> 164 us (1.012)
  Pallas kernels: 159 us -> 161 us
where the time goes in v3:
time: 164 us; the launch traced here: 163 us
  Pallas kernels  161 us (98%)
    pallas_call x1, Pallas kernels, body(): pl.pallas_call(functools.partial(halo_kernel, n_row, n_sub, stages, last)...  131 us
    pallas_call x1, Pallas kernels, body(): pl.pallas_call(block_kernel, out_shape=jax.ShapeDtypeStruct((n_blk, n_nbr...  29.8 us

profile of v3, /device:TPU:1, one launch (start us, length us, event | category | flops | bytes accessed | tf_op | source)
XLA Modules:
  0.0 162.7 jit_solution(4059511675448728765)
XLA Ops:
  0.0 0.7 fusion.listed
  0.7 0.0 copy-start
  0.7 0.7 copy-done
  1.4 0.0 copy-start.1
  1.4 0.7 copy-done.1
  2.1 130.8 %halo.1 = (f32[160,64,512]{2,1,0:T(8,128)}, bf16[16,512,256]{2,1,0:T(8,128)(2,1)S(1)}) custom-call(f32[32,64,512]{2,1,0:T(8,128)} %bitcast.8, f32[32,64,512]{2,1,0:T(8,128)} %bitcast.9, f32[1,512]{1,0:T(1,128)S(1)} %bitcast.5, s32[1,512]{1,0:T(1,128)S(1)} %bitcast.6), custom_call_target="tpu_custom_call" | custom-call | tf_op jit(solution)/shard_map/halo/pallas_call | solution.py:287
  132.9 29.8 %blocks.1 = f32[16,12,128,128]{3,2,1,0:T(8,128)} custom-call(s32[16,12]{1,0:T(8,128)S(1)} %fusion.listed, bf16[16,512,256]{2,1,0:T(8,128)(2,1)S(1)} %get-tuple-element.7.wcat, f32[80,128,512]{2,1,0:T(8,128)} %bitcast.7), custom_call_target="tpu_custom_call" | custom-call | tf_op jit(solution)/shard_map/blocks/pallas_call | solution.py:328
Async XLA Ops:
  0.7 0.7 copy-start
  1.4 0.7 copy-start.1

commit v4 on v3

--- a/solution.py
+++ b/solution.py
@@ -12,7 +12,7 @@
 CHUNK = 64
 WIN = 6
 LAG = 4
-GAP = 2
+GAP = 1
 
 broadening_sq = 0.0025
 MESH = pl.DeviceIdType.MESH
@@ -43,9 +43,9 @@
 
 
 def halo_kernel(n_row, n_sub, stages, last,
-                eig, cot, levels, order, table, wcat,
-                qv, vv, acc, full, recv, sh, sl, wv,
-                ld_sem, own_sem, w_sem, halo_send, halo_recv, ar_send, ar_recv):
+                eig, cot, levels, order, picks, table, wcat, early,
+                near, vv, ev, acc, full, recv, sh, sl, wv,
+                ld_sem, e_sem, w_sem, halo_send, halo_recv, ar_send, ar_recv):
     n_chunk = eig.shape[0]
     window = eig.shape[2]
     row = lax.axis_index("row")
@@ -72,17 +72,19 @@
     per = PIECE // CHUNK
     blocks = PIECE // BS
     n_piece = n_chunk // per
+    n_near = (near.shape[0] - n_chunk) // 4
+    n_far = n_chunk - n_near
+    n_blk = n_chunk * CHUNK // BS
+    two = BS // CHUNK
 
     def load(p, which):
-        src, dst = ((eig, qv), (cot, vv))[which]
+        src, dst = ((eig, near), (cot, vv))[which]
         at = pl.ds(p * per, per)
         return pltpu.make_async_copy(src.at[at], dst.at[at], ld_sem.at[which, p])
 
     for p in range(n_piece):
         load(p, 0).start()
         load(p, 1).start()
-    own = pltpu.make_async_copy(eig, table.at[pl.ds(0, n_chunk)], own_sem)
-    own.start()
 
     acc[...] = jnp.zeros_like(acc)
     for there in partners:
@@ -91,9 +93,14 @@
 
     def halo(way, t):
         dev = ((row, sub_up), (row, sub_down), (pair_row, sub), (ahead, sub))[way]
-        src = table.at[3 * n_chunk + t] if way == 3 else eig.at[t]
+        def place(way):
+            if t < n_near:
+                return near.at[n_chunk + way * n_near + t]
+            return table.at[way * n_far + t - n_near]
+
+        src = place(2) if way == 3 else eig.at[t]
         return pltpu.make_async_remote_copy(
-            src_ref=src, dst_ref=table.at[(way + 1) * n_chunk + t],
+            src_ref=src, dst_ref=place(way),
             send_sem=halo_send.at[way, t], recv_sem=halo_recv.at[way, t],
             device_id=dev, device_id_type=MESH)
 
@@ -102,7 +109,7 @@
             load(p, 0).wait()
             load(p, 1).wait()
             at = pl.ds(p * per, per)
-            qh, ql = split(qv[at].reshape(PIECE, window))
+            qh, ql = split(near[at].reshape(PIECE, window))
             vh, vl = split(vv[at].reshape(PIECE, window))
             d = ((0,), (0,))
             acc[...] += mm(qh, vh, d) + (mm(qh, vl, d) + mm(ql, vh, d))
@@ -160,7 +167,7 @@
 
     def adjoint(first, count):
         def body(p, carry):
-            qh, ql = split(qv[pl.ds(p * per, per)].reshape(PIECE, window))
+            qh, ql = split(near[pl.ds(p * per, per)].reshape(PIECE, window))
             d = ((1,), (0,))
             w = mm(qh, sh[...], d) + (mm(qh, sl[...], d) + mm(ql, sh[...], d))
             for b in range(blocks):
@@ -170,6 +177,37 @@
             return carry
 
         lax.fori_loop(first, first + count, body, 0)
+
+    def put_early(i):
+        return pltpu.make_async_copy(ev.at[i % 2], early.at[i], e_sem.at[i % 2])
+
+    def products(first, count):
+        n_nbr = ev.shape[1]
+        group = n_nbr // 2
+
+        def body(i, carry):
+            @pl.when(i >= 2)
+            def _():
+                put_early(i - 2).wait()
+
+            for g in range(0, n_nbr, group):
+                rows = [near[pl.ds(picks[i, g + k] * two, two)].reshape(BS, window) for k in range(group)]
+                qh, ql = split(jnp.concatenate(rows, axis=0))
+                d = ((1,), (0,))
+                big = mm(qh, wv[i], d)
+                res = big[:, :BS] + (big[:, BS:] + mm(ql, wv[i, :, :BS], d))
+                for k in range(group):
+                    ev[i % 2, g + k] = res[k * BS:(k + 1) * BS].T
+            put_early(i).start()
+            return carry
+
+        lax.fori_loop(first, first + count, body, 0)
+
+    def first_products(count):
+        for t in range(n_near):
+            for way in (0, 1, 3):
+                halo(way, t).wait_recv()
+        products(0, count)
 
     rounds = [k for k in range(len(stages)) if stages[k][3]]
     def begin():
@@ -212,6 +250,12 @@
     for p in range(0, n_piece, 2):
         at_step += 1
         jobs[at_step] = functools.partial(adjoint, p, 2)
+    at_step = max(at_step + 1, n_near + LAG + 1)
+    quarter = n_blk // 4
+    for p in range(0, n_blk, quarter):
+        jobs[at_step] = (functools.partial(products, p, quarter) if p
+                         else functools.partial(first_products, quarter))
+        at_step += 2
 
     for t in range(max(n_chunk + LAG, max(jobs) + 1)):
         if t < n_chunk:
@@ -230,46 +274,53 @@
 
     put = pltpu.make_async_copy(wv, wcat, w_sem)
     put.start()
-    for t in range(n_chunk):
+    for t in range(n_near, n_chunk):
         for way in (0, 1, 3):
             halo(way, t).wait_recv()
     for t in range(n_chunk - WIN, n_chunk):
         for way in (0, 1, 2, 3):
             halo(way, t).wait_send()
-    own.wait()
     put.wait()
-
-
-def block_kernel(listed, wcat, table, out, buf, sem):
+    put_early(n_blk - 2).wait()
+    put_early(n_blk - 1).wait()
+
+
+def block_kernel(late, wcat, early, table, out, buf, sem):
     i = pl.program_id(0)
     n = pl.num_programs(0)
     n_nbr = buf.shape[1]
-    window = table.shape[2]
+    d = ((1,), (0,))
 
     def fetch(step, k):
         slot = step % 2
-        return pltpu.make_async_copy(table.at[listed[step, k]], buf.at[slot, k], sem.at[slot, k])
+        at = jnp.maximum(late[step, k], 0)
+        return pltpu.make_async_copy(table.at[at], buf.at[slot, k], sem.at[slot, k])
+
+    def fetch_all(step):
+        for k in range(n_nbr):
+            @pl.when(late[step, k] >= 0)
+            def _():
+                fetch(step, k).start()
 
     @pl.when(i == 0)
     def _():
-        for k in range(n_nbr):
-            fetch(0, k).start()
+        fetch_all(0)
 
     @pl.when(i + 1 < n)
     def _():
-        for k in range(n_nbr):
-            fetch(i + 1, k).start()
-
-    d = ((1,), (0,))
+        fetch_all(i + 1)
+
     for k in range(n_nbr):
-        fetch(i, k).wait()
-    group = 4
-    for first in range(0, n_nbr, group):
-        qh, ql = split(buf[i % 2, pl.ds(first, group)].reshape(group * BS, window))
-        big = mm(qh, wcat[0], d)
-        res = big[:, :BS] + (big[:, BS:] + mm(ql, wcat[0, :, :BS], d))
-        for k in range(group):
-            out[0, first + k] = res[k * BS:(k + 1) * BS].T
+        @pl.when(late[i, k] >= 0)
+        def _():
+            fetch(i, k).wait()
+            qh, ql = split(buf[i % 2, k])
+            big = mm(qh, wcat[0], d)
+            out[0, k] = (big[:, :BS] + (big[:, BS:] + mm(ql, wcat[0, :, :BS], d))).T
+
+        @pl.when(late[i, k] < 0)
+        def _():
+            out[0, k] = early[0, k]
 
 
 def body(n_row, n_sub, eig_vectors, vec_cotangent, levels, order, neighbours):
@@ -284,17 +335,35 @@
     any_spec = pl.BlockSpec(memory_space=pl.ANY)
     vmem_spec = pl.BlockSpec(memory_space=pltpu.VMEM)
     n_st = len(stages)
-    table, wcat = pl.pallas_call(
+    near = n_blk * 5 // 8
+    far = n_blk - near
+    two = BS // CHUNK
+    my_row = lax.axis_index("row")
+    my_sub = lax.axis_index("sub")
+    device = neighbours // n_blk
+    local = neighbours % n_blk
+    dev_row = device // n_sub
+    dev_sub = device % n_sub
+    pair_row = my_row + 1 - 2 * (my_row % 2)
+    up = (my_sub + 1) % n_sub
+    same_row = jnp.where(dev_sub == my_sub, -1, jnp.where(dev_sub == up, 1, 0))
+    way = jnp.where(dev_row == my_row, same_row, jnp.where(dev_row == pair_row, 2, 3))
+    is_late = (way >= 0) & (local >= near)
+    picks = jnp.where(way < 0, local, jnp.where(is_late, 0, n_blk + way * near + local))
+    late = jnp.where(is_late, way * far + local - near, -1)
+    table, wcat, early = pl.pallas_call(
         functools.partial(halo_kernel, n_row, n_sub, stages, last),
         out_shape=[
-            jax.ShapeDtypeStruct((5 * n_chunk, CHUNK, window), F32),
+            jax.ShapeDtypeStruct((4 * far * two, CHUNK, window), F32),
             jax.ShapeDtypeStruct((n_blk, window, 2 * BS), BF16),
+            jax.ShapeDtypeStruct((n_blk, n_nbr, BS, BS), F32),
         ],
-        in_specs=[any_spec, any_spec, vmem_spec, vmem_spec],
-        out_specs=[any_spec, any_spec],
+        in_specs=[any_spec, any_spec, vmem_spec, vmem_spec, pl.BlockSpec(memory_space=pltpu.SMEM)],
+        out_specs=[any_spec, any_spec, any_spec],
         scratch_shapes=[
+            pltpu.VMEM((n_chunk + 4 * near * two, CHUNK, window), F32),
             pltpu.VMEM((n_chunk, CHUNK, window), F32),
-            pltpu.VMEM((n_chunk, CHUNK, window), F32),
+            pltpu.VMEM((2, n_nbr, BS, BS), F32),
             pltpu.VMEM((window, window), F32),
             pltpu.VMEM((window, window), F32),
             pltpu.VMEM((n_rec, window), F32),
@@ -302,7 +371,7 @@
             pltpu.VMEM((window, window), BF16),
             pltpu.VMEM((n_blk, window, 2 * BS), BF16),
             pltpu.SemaphoreType.DMA((2, rows // PIECE)),
-            pltpu.SemaphoreType.DMA,
+            pltpu.SemaphoreType.DMA((2,)),
             pltpu.SemaphoreType.DMA,
             pltpu.SemaphoreType.DMA((4, n_chunk)),
             pltpu.SemaphoreType.DMA((4, n_chunk)),
@@ -312,18 +381,8 @@
         compiler_params=pltpu.CompilerParams(
             collective_id=0, has_side_effects=True, vmem_limit_bytes=48 * 2**20),
         name="halo",
-    )(eig, cot, levels.reshape(1, window), order.reshape(1, window))
-
-    my_row = lax.axis_index("row")
-    my_sub = lax.axis_index("sub")
-    device = neighbours // n_blk
-    dev_row = device // n_sub
-    dev_sub = device % n_sub
-    pair_row = my_row + 1 - 2 * (my_row % 2)
-    up = (my_sub + 1) % n_sub
-    same_row = jnp.where(dev_sub == my_sub, 0, jnp.where(dev_sub == up, 2, 1))
-    slot = jnp.where(dev_row == my_row, same_row, jnp.where(dev_row == pair_row, 3, 4))
-    listed = slot * n_blk + neighbours % n_blk
+    )(eig, cot, levels.reshape(1, window), order.reshape(1, window),
+      picks.astype(jnp.int32))
 
     return pl.pallas_call(
         block_kernel,
@@ -332,10 +391,11 @@
             num_scalar_prefetch=1,
             grid=(n_blk,),
             in_specs=[
-                pl.BlockSpec((1, window, 2 * BS), lambda i, listed: (i, 0, 0)),
+                pl.BlockSpec((1, window, 2 * BS), lambda i, late: (i, 0, 0)),
+                pl.BlockSpec((1, n_nbr, BS, BS), lambda i, late: (i, 0, 0, 0)),
                 any_spec,
             ],
-            out_specs=pl.BlockSpec((1, n_nbr, BS, BS), lambda i, listed: (i, 0, 0, 0)),
+            out_specs=pl.BlockSpec((1, n_nbr, BS, BS), lambda i, late: (i, 0, 0, 0)),
             scratch_shapes=[
                 pltpu.VMEM((2, n_nbr, BS, window), F32),
                 pltpu.SemaphoreType.DMA((2, n_nbr)),
@@ -343,7 +403,7 @@
         ),
         compiler_params=pltpu.CompilerParams(vmem_limit_bytes=48 * 2**20),
         name="blocks",
-    )(listed.astype(jnp.int32), wcat, table.reshape(5 * n_blk, BS, window))
+    )(late.astype(jnp.int32), wcat, early, table.reshape(4 * far, BS, window))
 
 
 def solution(mesh):

time: 164 us -> 162 us (0.988)
  Pallas kernels: 161 us -> 157 us
    pallas_call x1, Pallas kernels: 29.8 us -> 25.6 us  [body(): pl.pallas_call(block_kernel, out_shape=jax.ShapeDtypeStruct((n_blk, n_nbr...]
where the time goes in v4:
time: 162 us; the launch traced here: 159 us
  Pallas kernels  157 us (97%)
    pallas_call x1, Pallas kernels, body(): pl.pallas_call(functools.partial(halo_kernel, n_row, n_sub, stages, last)...  132 us
    pallas_call x1, Pallas kernels, body(): pl.pallas_call(block_kernel, out_shape=jax.ShapeDtypeStruct((n_blk, n_nbr...  25.6 us

profile of v4, /device:TPU:1, one launch (start us, length us, event | category | flops | bytes accessed | tf_op | source)
XLA Modules:
  0.0 159.5 jit_solution(14852114043552002500)
XLA Ops:
  0.0 0.7 select_select_fusion
  0.7 0.0 copy-start
  0.7 0.7 copy-done
  1.4 0.0 copy-start.1
  1.4 0.7 copy-done.1
  2.1 131.7 %halo.1 = (f32[48,64,512]{2,1,0:T(8,128)}, bf16[16,512,256]{2,1,0:T(8,128)(2,1)S(1)}, f32[16,12,128,128]{3,2,1,0:T(8,128)}) custom-call(f32[32,64,512]{2,1,0:T(8,128)} %bitcast.8, f32[32,64,512]{2,1,0:T(8,128)} %bitcast.9, f32[1,512]{1,0:T(1,128)S(1)} %bitcast.5, s32[1,512]{1,0:T(1,128)S(1)} %bitcast.6, s32[16,12]{1,0:T(8,128)S(1)} %get-tuple-element.11.picks), custom_call_target="tpu_custom_call" | custom-call | tf_op jit(solution)/shard_map/halo/pallas_call | solution.py:354
  133.8 25.6 %blocks.1 = f32[16,12,128,128]{3,2,1,0:T(8,128)} custom-call(s32[16,12]{1,0:T(8,128)S(1)} %get-tuple-element.12.late, bf16[16,512,256]{2,1,0:T(8,128)(2,1)S(1)} %get-tuple-element.8.wcat, f32[16,12,128,128]{3,2,1,0:T(8,128)} %get-tuple-element.9.early, f32[24,128,512]{2,1,0:T(8,128)} %bitcast.7), custom_call_target="tpu_custom_call" | custom-call | tf_op jit(solution)/shard_map/blocks/pallas_call | solution.py:387
Async XLA Ops:
  0.7 0.7 copy-start
  1.4 0.7 copy-start.1
